TPU v7x, 512 devices: a whole 4x4x16 slice. The times are simulated.
512 devices in a mesh: dp: 4 (over x), expert: 128 (over z, y, core).
Axes of the slice: x: 4, y: 4, z: 16, core: 2. Of those that a mesh axis runs over, the one named last changes fastest.
Arguments:
- tokens: bfloat16 [8192, 2048], P(('dp', 'expert')), may hold values from -6 to 6
- cotangent: bfloat16 [8192, 2048], P(('dp', 'expert')), may hold values from -6 to 6
- expert_ids: int32 [8192, 8], P(('dp', 'expert')), may hold values from 0 to 127, all different within a row; in each aligned block of 16 rows (0 to 15, 16 to 31, ...) at most 2 rows name the same one
- gate_values: float32 [8192, 8], P(('dp', 'expert')), may hold values from 0.05 to 0.5
- gate_weight: bfloat16 [128, 2048, 384], P('expert', 'dp'), may hold values from -0.125 to 0.125
- up_weight: bfloat16 [128, 2048, 384], P('expert', 'dp'), may hold values from -0.125 to 0.125
- down_weight: bfloat16 [128, 2048, 384], P('expert', 'dp'), may hold values from -0.3125 to 0.3125
Outputs:
- mixed: bfloat16 [8192, 2048], P(('dp', 'expert'))
- input_grad: bfloat16 [8192, 2048], P(('dp', 'expert'))
- gate_grad: float32 [8192, 8], P(('dp', 'expert'))
- gate_weight_grad: float32 [128, 2048, 384], P('expert', 'dp')
- up_weight_grad: float32 [128, 2048, 384], P('expert', 'dp')
Inputs may be any that keep to these rules, and one draw needn't show every extreme that they name: `expert_ids`: each row names 8 different experts. Among the 16 rows of one device no expert is named more than 2 times.
All inputs are finite; a program needn't handle non-finite values.
Results may differ from a plain program's by a relative error of at most 0.012.
Values may be sent and summed in bfloat16 or wider, within the bound.
A program may use at most 64 MiB of HBM per device.

v0:
```python
import jax
import jax.numpy as jnp
from jax import lax
from jax.sharding import PartitionSpec as P


def body(tokens, cotangent, expert_ids, gate_values, gate_weight, up_weight, down_weight):
    tok_rows = tokens.shape[0]
    feature_width = tokens.shape[1]
    top_count = expert_ids.shape[1]
    experts = lax.axis_size("expert")
    routed = tok_rows * top_count
    capacity = min(tok_rows, max(2, (routed + experts - 1) // experts + 1))
    flat_ids = expert_ids.reshape(routed)
    onehot = (flat_ids[:, None] == jnp.arange(experts, dtype=jnp.int32)[None, :]).astype(jnp.int32)
    earlier = jnp.cumsum(onehot, axis=0) - onehot
    slot_rank = jnp.sum(earlier * onehot, axis=1)
    target = flat_ids * capacity + slot_rank
    owner_row = jnp.arange(routed, dtype=jnp.int32) // top_count
    gate_flat = gate_values.reshape(routed)
    picked = tokens[owner_row]
    scaled = (gate_flat[:, None] * cotangent[owner_row].astype(jnp.float32)).astype(jnp.bfloat16)
    slot_count = experts * capacity
    send_rows = jnp.zeros((slot_count, feature_width), jnp.bfloat16).at[target].set(picked)
    send_rows = send_rows.reshape(experts, capacity, feature_width)
    send_grads = jnp.zeros((slot_count, feature_width), jnp.bfloat16).at[target].set(scaled)
    send_grads = send_grads.reshape(experts, capacity, feature_width)
    gate_full, up_full, down_full = (
        lax.all_gather(gate_weight, "dp", axis=1, tiled=True),
        lax.all_gather(up_weight, "dp", axis=1, tiled=True),
        lax.all_gather(down_weight, "dp", axis=1, tiled=True),
    )
    gate_mat = gate_full[0]
    up_mat = up_full[0]
    arrived = lax.all_to_all(send_rows, "expert", split_axis=0, concat_axis=0, tiled=True)
    rows = arrived.reshape(slot_count, feature_width)
    hidden_gate = jnp.dot(rows, gate_mat, preferred_element_type=jnp.float32)
    hidden_up = jnp.dot(rows, up_mat, preferred_element_type=jnp.float32)
    down_mat = down_full[0]
    sigma = jax.nn.sigmoid(hidden_gate)
    active = (hidden_gate * sigma * hidden_up).astype(jnp.bfloat16)
    contract_last = (((1,), (1,)), ((), ()))
    outputs = lax.dot_general(
        active, down_mat, contract_last, preferred_element_type=jnp.float32
    ).astype(jnp.bfloat16)
    outputs = outputs.reshape(experts, capacity, feature_width)
    returned = lax.all_to_all(outputs, "expert", split_axis=0, concat_axis=0, tiled=True)
    arrived_grads = lax.all_to_all(send_grads, "expert", split_axis=0, concat_axis=0, tiled=True)
    grad_rows = arrived_grads.reshape(slot_count, feature_width)
    grad_active = jnp.dot(grad_rows, down_mat, preferred_element_type=jnp.float32)
    grad_up = (grad_active * hidden_gate * sigma).astype(jnp.bfloat16)
    grad_gate = (grad_active * hidden_up * sigma * (1.0 + hidden_gate * (1.0 - sigma))).astype(
        jnp.bfloat16
    )
    input_rows = lax.dot_general(
        grad_gate, gate_mat, contract_last, preferred_element_type=jnp.float32
    )
    input_rows = input_rows + lax.dot_general(
        grad_up, up_mat, contract_last, preferred_element_type=jnp.float32
    )
    input_rows = input_rows.astype(jnp.bfloat16).reshape(experts, capacity, feature_width)
    returned_grads = lax.all_to_all(input_rows, "expert", split_axis=0, concat_axis=0, tiled=True)
    contract_rows = (((0,), (0,)), ((), ()))
    gate_part = lax.dot_general(rows, grad_gate, contract_rows, preferred_element_type=jnp.float32)
    up_part = lax.dot_general(rows, grad_up, contract_rows, preferred_element_type=jnp.float32)
    gate_weight_grad, up_weight_grad = (
        lax.psum_scatter(
            gate_part[None].astype(jnp.bfloat16), "dp", scatter_dimension=1, tiled=True
        ).astype(jnp.float32),
        lax.psum_scatter(
            up_part[None].astype(jnp.bfloat16), "dp", scatter_dimension=1, tiled=True
        ).astype(jnp.float32),
    )
    back_rows = returned.reshape(slot_count, feature_width)[target].astype(jnp.float32)
    back_rows = back_rows.reshape(tok_rows, top_count, feature_width)
    back_grads = returned_grads.reshape(slot_count, feature_width)[target].astype(jnp.float32)
    back_grads = back_grads.reshape(tok_rows, top_count, feature_width)
    weights_here = gate_flat.reshape(tok_rows, top_count)
    mixed = jnp.sum(weights_here[:, :, None] * back_rows, axis=1).astype(jnp.bfloat16)
    gate_grad = jnp.sum(back_rows * cotangent.astype(jnp.float32)[:, None, :], axis=2)
    input_grad = jnp.sum(back_grads, axis=1).astype(jnp.bfloat16)
    return (mixed, input_grad, gate_grad, gate_weight_grad, up_weight_grad)


def solution(mesh):
    placed = (
        P(("dp", "expert"), None),
        P(("dp", "expert"), None),
        P(("dp", "expert"), None),
        P(("dp", "expert"), None),
        P("expert", "dp", None),
        P("expert", "dp", None),
        P("expert", "dp", None),
    )
    return jax.shard_map(
        body,
        mesh=mesh,
        in_specs=placed,
        out_specs=(
            P(("dp", "expert"), None),
            P(("dp", "expert"), None),
            P(("dp", "expert"), None),
            P("expert", "dp", None),
            P("expert", "dp", None),
        ),
        check_vma=False,
    )
```

profile of v0, /device:TPU:33, one launch (start us, length us, event | category | flops | bytes accessed | tf_op | source)
XLA Modules:
  0.0 292.1 jit_solution(706173469473217055)
XLA Ops:
  7.2 0.7 broadcast_multiply_fusion
  7.9 0.8 copy.22
  8.8 0.1 eq.15
  8.9 0.1 fusion.22
  9.0 0.2 reduce_window_sum.11
  9.2 0.2 select_reduce_fusion
  9.4 3.4 %scatter_custom_fusion = bf16[256,2048]{1,0:T(8,128)(2,1)S(1)} fusion(s32[128]{0:T(128)S(1)} %fusion.24, bf16[16,2048]{1,0:T(8,128)(2,1)S(1)} %copy-done, s32[1024]{0:T(1024)S(1)} %pad_clamp_fusion.1, bf16[]{:T(256)} %constant.26.clone.1), kind=kCustom, calls=%fused_computation.30 | custom fusion | bytes 1048578 | tf_op jit(solution)/shard_map/scatter | solution.py:24
  12.8 1.5 reshape.128
  14.3 19.6 %all-to-all-start = ((bf16[128,2,2048]{2,1,0:T(2,128)(2,1)}), bf16[128,2,2048]{2,1,0:T(2,128)(2,1)S(1)}, u32[]{:S(2)}, u32[]{:S(2)}) async-start(bf16[128,2,2048]{2,1,0:T(2,128)(2,1)} %reshape.128), calls=%async_computation | async-start | bytes 2097152 | tf_op jit(solution)/shard_map/all_to_all | solution.py:35
  33.9 0.7 all-gather.6.cloned.1.call-update
  34.7 0.7 all-gather.4.cloned.1.call-update
  35.6 3.4 %scatter_custom_fusion.1 = bf16[256,2048]{1,0:T(8,128)(2,1)S(1)} fusion(s32[128]{0:T(128)S(1)} %fusion.24, f32[128]{0:T(128)S(1)} %mul.81, bf16[]{:T(256)} %constant.26.clone.1, bf16[16,2048]{1,0:T(8,128)(2,1)S(1)} %copy-done.3, s32[1024]{0:T(1024)S(1)} %pad_clamp_fusion.1), kind=kCustom, calls=%fused_computation.28 | custom fusion | flops 786432 | bytes 1118722 | tf_op jit(solution)/shard_map/scatter | solution.py:26
  39.0 1.5 reshape.132
  40.5 49.0 %all-to-all-done = bf16[128,2,2048]{2,1,0:T(2,128)(2,1)S(1)} async-done(((bf16[128,2,2048]{2,1,0:T(2,128)(2,1)}), bf16[128,2,2048]{2,1,0:T(2,128)(2,1)S(1)}, u32[]{:S(2)}, u32[]{:S(2)}) %all-to-all-start) | async-done | bytes 1048608 | tf_op jit(solution)/shard_map/all_to_all | solution.py:35
  89.5 6.4 %all-to-all-start.2 = ((bf16[128,2,2048]{2,1,0:T(2,128)(2,1)}), bf16[128,2,2048]{2,1,0:T(2,128)(2,1)S(1)}, u32[]{:S(2)}, u32[]{:S(2)}) async-start(bf16[128,2,2048]{2,1,0:T(2,128)(2,1)} %reshape.132), calls=%async_computation.2 | async-start | bytes 2097152 | tf_op jit(solution)/shard_map/all_to_all | solution.py:48
  96.0 0.2 all-gather.8.cloned.1.call-start
  96.2 0.5 all-gather.8.cloned.1.call-update
  96.7 0.4 reshape.129
  97.2 2.9 fusion.7
  100.0 8.2 %all-gather.4.cloned.1.call-done = bf16[1,2048,384]{2,1,0:T(8,128)(2,1)} async-done(((bf16[1,512,384]{2,1,0:T(8,128)(2,1)}), bf16[1,2048,384]{2,1,0:T(8,128)(2,1)}) %all-gather.4.cloned.1.call-update) | async-done | bytes 1572880 | tf_op jit(solution)/shard_map/all_gather | solution.py:29
  108.2 2.9 fusion.11
  111.1 33.6 %all-gather.8.cloned.1.call-done = bf16[1,2048,384]{2,1,0:T(8,128)(2,1)} async-done(((bf16[1,512,384]{2,1,0:T(8,128)(2,1)}), bf16[1,2048,384]{2,1,0:T(8,128)(2,1)}) %all-gather.8.cloned.1.call-update) | async-done | bytes 1572880 | tf_op jit(solution)/shard_map/all_gather | solution.py:31
  144.7 2.4 convolution_convert_fusion.2
  147.1 1.5 reshape.130
  148.6 2.9 %all-to-all-done.2 = bf16[128,2,2048]{2,1,0:T(2,128)(2,1)S(1)} async-done(((bf16[128,2,2048]{2,1,0:T(2,128)(2,1)}), bf16[128,2,2048]{2,1,0:T(2,128)(2,1)S(1)}, u32[]{:S(2)}, u32[]{:S(2)}) %all-to-all-start.2) | async-done | bytes 1048608 | tf_op jit(solution)/shard_map/all_to_all | solution.py:48
  151.6 14.3 %all-to-all-start.1 = ((bf16[128,2,2048]{2,1,0:T(2,128)(2,1)}), bf16[128,2,2048]{2,1,0:T(2,128)(2,1)}, u32[]{:S(2)}, u32[]{:S(2)}) async-start(bf16[128,2,2048]{2,1,0:T(2,128)(2,1)} %reshape.130), calls=%async_computation.1 | async-start | bytes 2097152 | tf_op jit(solution)/shard_map/all_to_all | solution.py:47
  165.9 0.4 reshape.133
  166.4 2.4 multiply_convert_fusion.2
  168.7 1.9 fusion
  170.7 0.7 fusion.9
  171.4 0.7 copy-done.1
  172.1 0.8 fusion.2
  172.9 1.5 reshape.134
  174.4 46.8 %all-to-all-done.1 = bf16[128,2,2048]{2,1,0:T(2,128)(2,1)} async-done(((bf16[128,2,2048]{2,1,0:T(2,128)(2,1)}), bf16[128,2,2048]{2,1,0:T(2,128)(2,1)}, u32[]{:S(2)}, u32[]{:S(2)}) %all-to-all-start.1) | async-done | bytes 1048608 | tf_op jit(solution)/shard_map/all_to_all | solution.py:47
  221.1 6.4 %all-to-all-start.3 = ((bf16[128,2,2048]{2,1,0:T(2,128)(2,1)}), bf16[128,2,2048]{2,1,0:T(2,128)(2,1)S(1)}, u32[]{:S(2)}, u32[]{:S(2)}) async-start(bf16[128,2,2048]{2,1,0:T(2,128)(2,1)} %reshape.134), calls=%async_computation.3 | async-start | bytes 2097152 | tf_op jit(solution)/shard_map/all_to_all | solution.py:62
  227.6 0.3 reduce-scatter.5.cloned.1.call-start
  227.8 1.9 fusion.1
  229.8 1.9 convert_element_type.76
  231.8 31.1 %reduce-scatter.5.cloned.1.call-done = bf16[1,512,384]{2,1,0:T(8,128)(2,1)} async-done(((bf16[1,2048,384]{2,1,0:T(8,128)(2,1)}), bf16[1,512,384]{2,1,0:T(8,128)(2,1)}) %reduce-scatter.5.cloned.1.call-update) | async-done | bytes 393232 | tf_op jit(solution)/shard_map/reduce_scatter | solution.py:70
  262.8 1.9 convert_element_type.79
  264.8 1.5 reshape.131
  266.2 0.9 gather_fusion
  267.2 1.7 fusion.14
  268.9 0.7 copy.24
  269.5 13.7 %all-to-all-done.3 = bf16[128,2,2048]{2,1,0:T(2,128)(2,1)S(1)} async-done(((bf16[128,2,2048]{2,1,0:T(2,128)(2,1)}), bf16[128,2,2048]{2,1,0:T(2,128)(2,1)S(1)}, u32[]{:S(2)}, u32[]{:S(2)}) %all-to-all-start.3) | async-done | bytes 1048608 | tf_op jit(solution)/shard_map/all_to_all | solution.py:62
  283.2 0.4 reshape.135
  283.6 0.9 gather_fusion.1
  284.6 1.0 bitcast_reduce_fusion
  (25 shorter events, 0.6 us)
Async XLA Ops:
  7.2 2.2 copy-start
  14.3 21.1 %copy-start.4 = (f32[16,8]{0,1:T(8,128)S(1)}, f32[16,8]{0,1:T(8,128)}, u32[]{:S(2)}) copy-start(f32[16,8]{0,1:T(8,128)} %param.10) | copy-start | bytes 1540
  14.3 21.3 %copy-start.3 = (bf16[16,2048]{1,0:T(8,128)(2,1)S(1)}, bf16[16,2048]{1,0:T(8,128)(2,1)}, u32[]{:S(2)}) copy-start(bf16[16,2048]{1,0:T(8,128)(2,1)} %param.8) | copy-start | bytes 196612
  14.3 75.2 %all-to-all-start = ((bf16[128,2,2048]{2,1,0:T(2,128)(2,1)}), bf16[128,2,2048]{2,1,0:T(2,128)(2,1)S(1)}, u32[]{:S(2)}, u32[]{:S(2)}) async-start(bf16[128,2,2048]{2,1,0:T(2,128)(2,1)} %reshape.128), calls=%async_computation | async-start | bytes 2097152 | tf_op jit(solution)/shard_map/all_to_all | solution.py:35
  33.9 63.3 %all-gather.6.cloned.1.call-start = ((), (), s32[]{:S(2)}) async-start(), calls=%async_computation.7 | async-start | bytes 1966080 | tf_op jit(solution)/shard_map/all_gather | solution.py:30
  34.6 73.6 %all-gather.4.cloned.1.call-start = ((), (), s32[]{:S(2)}) async-start(), calls=%async_computation.6 | async-start | bytes 1966080 | tf_op jit(solution)/shard_map/all_gather | solution.py:29
  89.5 62.1 %all-to-all-start.2 = ((bf16[128,2,2048]{2,1,0:T(2,128)(2,1)}), bf16[128,2,2048]{2,1,0:T(2,128)(2,1)S(1)}, u32[]{:S(2)}, u32[]{:S(2)}) async-start(bf16[128,2,2048]{2,1,0:T(2,128)(2,1)} %reshape.132), calls=%async_computation.2 | async-start | bytes 2097152 | tf_op jit(solution)/shard_map/all_to_all | solution.py:48
  96.0 48.7 %all-gather.8.cloned.1.call-start = ((), (), s32[]{:S(2)}) async-start(), calls=%async_computation.8 | async-start | bytes 1966080 | tf_op jit(solution)/shard_map/all_gather | solution.py:31
  151.6 69.6 %all-to-all-start.1 = ((bf16[128,2,2048]{2,1,0:T(2,128)(2,1)}), bf16[128,2,2048]{2,1,0:T(2,128)(2,1)}, u32[]{:S(2)}, u32[]{:S(2)}) async-start(bf16[128,2,2048]{2,1,0:T(2,128)(2,1)} %reshape.130), calls=%async_computation.1 | async-start | bytes 2097152 | tf_op jit(solution)/shard_map/all_to_all | solution.py:47
  165.9 64.0 %reduce-scatter.3.cloned.1.call-start = ((), (), s32[]{:S(2)}) async-start(), calls=%async_computation.9 | async-start | bytes 1966080 | tf_op jit(solution)/shard_map/reduce_scatter | solution.py:67
  168.7 1.9 copy-start.2
  170.7 1.4 copy-start.1
  221.1 62.1 %all-to-all-start.3 = ((bf16[128,2,2048]{2,1,0:T(2,128)(2,1)}), bf16[128,2,2048]{2,1,0:T(2,128)(2,1)S(1)}, u32[]{:S(2)}, u32[]{:S(2)}) async-start(bf16[128,2,2048]{2,1,0:T(2,128)(2,1)} %reshape.134), calls=%async_computation.3 | async-start | bytes 2097152 | tf_op jit(solution)/shard_map/all_to_all | solution.py:62
  227.6 35.3 %reduce-scatter.5.cloned.1.call-start = ((), (), s32[]{:S(2)}) async-start(), calls=%async_computation.10 | async-start | bytes 1966080 | tf_op jit(solution)/shard_map/reduce_scatter | solution.py:70
Sparse Core Ops, SparseCore 0:
  36.8 34.8 all-gather.5
  73.9 34.3 all-gather.3
  110.3 34.3 all-gather.7
  170.8 31.8 reduce-scatter.2
  230.9 31.8 reduce-scatter.4
where the time goes:
time: 293 us; the launch traced here: 292 us
  waiting for transfers between devices  187 us (64%)
  starting transfers between devices  47.4 us (16%)
  local copies, waits for them, and re-layouts  16.5 us (6%)
  matrix products  15.8 us (5%)
  between operations  14 us (5%)
  other arithmetic  11.1 us (4%)
    all_to_all x1, waiting for transfers between devices, body(): lax.all_to_all(send_rows, 'expert', split_axis=0, concat_axis=0, tiled=True)  49 us
    all_to_all x1, waiting for transfers between devices, body(): lax.all_to_all(outputs, 'expert', split_axis=0, concat_axis=0, tiled=True)  46.8 us
    all_gather x1, waiting for transfers between devices, body(): lax.all_gather(down_weight, 'dp', axis=1, tiled=True)  33.6 us
    reduce_scatter x1, waiting for transfers between devices, body(): lax.psum_scatter(up_part[None].astype(jnp.bfloat16), 'dp', scatter_dimens...  31.1 us
    all_to_all x1, starting transfers between devices, body(): lax.all_to_all(send_rows, 'expert', split_axis=0, concat_axis=0, tiled=True)  19.6 us
    all_to_all x1, starting transfers between devices, body(): lax.all_to_all(outputs, 'expert', split_axis=0, concat_axis=0, tiled=True)  14.3 us
    all_to_all x1, waiting for transfers between devices, body(): lax.all_to_all(input_rows, 'expert', split_axis=0, concat_axis=0, tiled=T...  13.7 us
    all_gather x1, waiting for transfers between devices, body(): lax.all_gather(gate_weight, 'dp', axis=1, tiled=True)  8.2 us
  transfers between devices with their start and end apart: 9, of which 7 were waited for; matrix products, arithmetic and copies ran while one was open for 11% of the time, Pallas kernels for 0%

commit v1 on v0

--- a/solution.py
+++ b/solution.py
@@ -28,7 +28,9 @@
     gate_full, up_full, down_full = (
         lax.all_gather(gate_weight, "dp", axis=1, tiled=True),
         lax.all_gather(up_weight, "dp", axis=1, tiled=True),
-        lax.all_gather(down_weight, "dp", axis=1, tiled=True),
+        jnp.concatenate(
+            lax.all_to_all(jnp.stack([down_weight] * lax.axis_size("dp")), "dp", 0, 0), axis=1
+        ),
     )
     gate_mat = gate_full[0]
     up_mat = up_full[0]

time: 293 us -> 309 us (1.055)
  waiting for transfers between devices: 187 us -> 205 us
  local copies, waits for them, and re-layouts: 16.5 us -> 20.1 us
    all_gather x1 -> x0, waiting for transfers between devices: 33.6 us -> none  [body(): lax.all_gather(down_weight, 'dp', axis=1, tiled=True)]
    all_gather x1, waiting for transfers between devices: 8.2 us -> 31.9 us  [body(): lax.all_gather(gate_weight, 'dp', axis=1, tiled=True)]
    all_to_all x0 -> x1, waiting for transfers between devices: none -> 14.1 us  [body(): lax.all_to_all(jnp.stack([down_weight] * lax.axis_size('dp')), 'dp', 0, 0)]
    all_to_all x1, waiting for transfers between devices: 2.94 us -> 14.3 us  [body(): lax.all_to_all(send_grads, 'expert', split_axis=0, concat_axis=0, tiled=T...]
    all_to_all x1, starting transfers between devices: 14.3 us -> 6.9 us  [body(): lax.all_to_all(outputs, 'expert', split_axis=0, concat_axis=0, tiled=True)]
    all_to_all x0 -> x1, starting transfers between devices: none -> 4.14 us  [body(): lax.all_to_all(jnp.stack([down_weight] * lax.axis_size('dp')), 'dp', 0, 0)]
where the time goes in v1:
time: 309 us; the launch traced here: 308 us
  waiting for transfers between devices  205 us (66%)
  starting transfers between devices  45.2 us (15%)
  local copies, waits for them, and re-layouts  20.1 us (7%)
  between operations  14 us (5%)
  matrix products  13.5 us (4%)
  other arithmetic  10.4 us (3%)
    all_to_all x1, waiting for transfers between devices, body(): lax.all_to_all(send_rows, 'expert', split_axis=0, concat_axis=0, tiled=True)  49.7 us
    all_to_all x1, waiting for transfers between devices, body(): lax.all_to_all(outputs, 'expert', split_axis=0, concat_axis=0, tiled=True)  46.8 us
    all_gather x1, waiting for transfers between devices, body(): lax.all_gather(gate_weight, 'dp', axis=1, tiled=True)  31.9 us
    reduce_scatter x1, waiting for transfers between devices, body(): lax.psum_scatter(up_part[None].astype(jnp.bfloat16), 'dp', scatter_dimens...  30.4 us
    all_to_all x1, starting transfers between devices, body(): lax.all_to_all(send_rows, 'expert', split_axis=0, concat_axis=0, tiled=True)  20.7 us
    all_to_all x1, waiting for transfers between devices, body(): lax.all_to_all(input_rows, 'expert', split_axis=0, concat_axis=0, tiled=T...  16.7 us
    all_to_all x1, waiting for transfers between devices, body(): lax.all_to_all(send_grads, 'expert', split_axis=0, concat_axis=0, tiled=T...  14.3 us
    all_to_all x1, waiting for transfers between devices, body(): lax.all_to_all(jnp.stack([down_weight] * lax.axis_size('dp')), 'dp', 0, 0)  14.1 us
  transfers between devices with their start and end apart: 9, of which 7 were waited for; matrix products, arithmetic and copies ran while one was open for 11% of the time, Pallas kernels for 0%

profile of v1, /device:TPU:33, one launch (start us, length us, event | category | flops | bytes accessed | tf_op | source)
XLA Modules:
  0.0 308.4 jit_solution(16272077377600392017)
XLA Ops:
  7.2 2.3 stack.2
  9.5 4.1 %all-to-all-start.1 = ((bf16[4,1,512,384]{3,2,1,0:T(8,128)(2,1)}), bf16[4,1,512,384]{3,2,1,0:T(8,128)(2,1)S(1)}, u32[]{:S(2)}, u32[]{:S(2)}) async-start(bf16[4,1,512,384]{3,2,1,0:T(8,128)(2,1)} %stack.2), calls=%async_computation.1 | async-start | bytes 3145728 | tf_op jit(solution)/shard_map/all_to_all | solution.py:32
  14.0 0.1 fusion.19
  14.1 0.2 reduce_window_sum.11
  14.3 0.2 select_reduce_fusion
  14.5 3.4 %scatter_custom_fusion = bf16[256,2048]{1,0:T(8,128)(2,1)S(1)} fusion(s32[128]{0:T(128)S(1)} %fusion.21, bf16[16,2048]{1,0:T(8,128)(2,1)S(1)} %copy-done, s32[1024]{0:T(1024)S(1)} %pad_clamp_fusion.1, bf16[]{:T(256)} %constant.26.clone.1), kind=kCustom, calls=%fused_computation.27 | custom fusion | bytes 1048578 | tf_op jit(solution)/shard_map/scatter | solution.py:24
  17.8 1.5 reshape.131
  19.3 14.1 %all-to-all-done.1 = bf16[4,1,512,384]{3,2,1,0:T(8,128)(2,1)S(1)} async-done(((bf16[4,1,512,384]{3,2,1,0:T(8,128)(2,1)}), bf16[4,1,512,384]{3,2,1,0:T(8,128)(2,1)S(1)}, u32[]{:S(2)}, u32[]{:S(2)}) %all-to-all-start.1) | async-done | bytes 1572896 | tf_op jit(solution)/shard_map/all_to_all | solution.py:32
  33.4 1.1 copy-done.3
  34.6 20.7 %all-to-all-start = ((bf16[128,2,2048]{2,1,0:T(2,128)(2,1)}), bf16[128,2,2048]{2,1,0:T(2,128)(2,1)S(1)}, u32[]{:S(2)}, u32[]{:S(2)}) async-start(bf16[128,2,2048]{2,1,0:T(2,128)(2,1)} %reshape.131), calls=%async_computation | async-start | bytes 2097152 | tf_op jit(solution)/shard_map/all_to_all | solution.py:37
  55.3 0.7 all-gather.5.cloned.1.call-update
  56.2 3.4 %scatter_custom_fusion.1 = bf16[256,2048]{1,0:T(8,128)(2,1)S(1)} fusion(s32[128]{0:T(128)S(1)} %fusion.21, f32[128]{0:T(128)S(1)} %mul.81, bf16[]{:T(256)} %constant.26.clone.1, bf16[16,2048]{1,0:T(8,128)(2,1)S(1)} %copy-done.7, s32[1024]{0:T(1024)S(1)} %pad_clamp_fusion.1), kind=kCustom, calls=%fused_computation.25 | custom fusion | flops 786432 | bytes 1118722 | tf_op jit(solution)/shard_map/scatter | solution.py:26
  59.6 1.5 reshape.135
  61.1 49.7 %all-to-all-done = bf16[128,2,2048]{2,1,0:T(2,128)(2,1)S(1)} async-done(((bf16[128,2,2048]{2,1,0:T(2,128)(2,1)}), bf16[128,2,2048]{2,1,0:T(2,128)(2,1)S(1)}, u32[]{:S(2)}, u32[]{:S(2)}) %all-to-all-start) | async-done | bytes 1048608 | tf_op jit(solution)/shard_map/all_to_all | solution.py:37
  110.9 6.4 %all-to-all-start.3 = ((bf16[128,2,2048]{2,1,0:T(2,128)(2,1)}), bf16[128,2,2048]{2,1,0:T(2,128)(2,1)S(1)}, u32[]{:S(2)}, u32[]{:S(2)}) async-start(bf16[128,2,2048]{2,1,0:T(2,128)(2,1)} %reshape.135), calls=%async_computation.3 | async-start | bytes 2097152 | tf_op jit(solution)/shard_map/all_to_all | solution.py:50
  117.3 0.2 all-gather.3.cloned.1.call-start
  117.6 0.5 all-gather.3.cloned.1.call-update
  118.1 0.4 reshape.132
  118.6 2.9 fusion.4
  121.4 31.9 %all-gather.3.cloned.1.call-done = bf16[1,2048,384]{2,1,0:T(8,128)(2,1)} async-done(((bf16[1,512,384]{2,1,0:T(8,128)(2,1)}), bf16[1,2048,384]{2,1,0:T(8,128)(2,1)}) %all-gather.3.cloned.1.call-update) | async-done | bytes 1572880 | tf_op jit(solution)/shard_map/all_gather | solution.py:29
  153.4 2.3 fusion.8
  155.6 0.7 copy-done.6
  156.4 0.8 convolution_convert_fusion.2
  157.1 1.5 reshape.133
  158.7 14.3 %all-to-all-done.3 = bf16[128,2,2048]{2,1,0:T(2,128)(2,1)S(1)} async-done(((bf16[128,2,2048]{2,1,0:T(2,128)(2,1)}), bf16[128,2,2048]{2,1,0:T(2,128)(2,1)S(1)}, u32[]{:S(2)}, u32[]{:S(2)}) %all-to-all-start.3) | async-done | bytes 1048608 | tf_op jit(solution)/shard_map/all_to_all | solution.py:50
  172.9 6.9 %all-to-all-start.2 = ((bf16[128,2,2048]{2,1,0:T(2,128)(2,1)}), bf16[128,2,2048]{2,1,0:T(2,128)(2,1)}, u32[]{:S(2)}, u32[]{:S(2)}) async-start(bf16[128,2,2048]{2,1,0:T(2,128)(2,1)} %reshape.133), calls=%async_computation.2 | async-start | bytes 2097152 | tf_op jit(solution)/shard_map/all_to_all | solution.py:49
  179.9 0.4 reshape.136
  180.3 2.4 multiply_convert_fusion.2
  182.7 1.9 fusion
  184.7 0.7 fusion.6
  185.4 0.7 copy-done.1
  186.1 0.8 fusion.2
  186.8 1.5 reshape.137
  188.3 46.8 %all-to-all-done.2 = bf16[128,2,2048]{2,1,0:T(2,128)(2,1)} async-done(((bf16[128,2,2048]{2,1,0:T(2,128)(2,1)}), bf16[128,2,2048]{2,1,0:T(2,128)(2,1)}, u32[]{:S(2)}, u32[]{:S(2)}) %all-to-all-start.2) | async-done | bytes 1048608 | tf_op jit(solution)/shard_map/all_to_all | solution.py:49
  235.1 6.4 %all-to-all-start.4 = ((bf16[128,2,2048]{2,1,0:T(2,128)(2,1)}), bf16[128,2,2048]{2,1,0:T(2,128)(2,1)S(1)}, u32[]{:S(2)}, u32[]{:S(2)}) async-start(bf16[128,2,2048]{2,1,0:T(2,128)(2,1)} %reshape.137), calls=%async_computation.4 | async-start | bytes 2097152 | tf_op jit(solution)/shard_map/all_to_all | solution.py:64
  241.6 0.3 reduce-scatter.5.cloned.1.call-start
  241.8 1.9 fusion.1
  243.8 1.9 convert_element_type.76
  245.7 30.4 %reduce-scatter.5.cloned.1.call-done = bf16[1,512,384]{2,1,0:T(8,128)(2,1)} async-done(((bf16[1,2048,384]{2,1,0:T(8,128)(2,1)}), bf16[1,512,384]{2,1,0:T(8,128)(2,1)}) %reduce-scatter.5.cloned.1.call-update) | async-done | bytes 393232 | tf_op jit(solution)/shard_map/reduce_scatter | solution.py:72
  276.1 1.9 convert_element_type.79
  278.1 1.5 reshape.134
  279.5 0.9 gather_fusion
  280.5 16.7 %all-to-all-done.4 = bf16[128,2,2048]{2,1,0:T(2,128)(2,1)S(1)} async-done(((bf16[128,2,2048]{2,1,0:T(2,128)(2,1)}), bf16[128,2,2048]{2,1,0:T(2,128)(2,1)S(1)}, u32[]{:S(2)}, u32[]{:S(2)}) %all-to-all-start.4) | async-done | bytes 1048608 | tf_op jit(solution)/shard_map/all_to_all | solution.py:64
  297.2 0.4 reshape.138
  297.6 0.9 gather_fusion.1
  298.5 1.0 bitcast_reduce_fusion
  299.5 1.7 fusion.11
  301.2 0.7 copy.24
  (35 shorter events, 0.7 us)
Async XLA Ops:
  7.2 7.3 %copy-start = (bf16[16,2048]{1,0:T(8,128)(2,1)S(1)}, bf16[16,2048]{1,0:T(8,128)(2,1)}, u32[]{:S(2)}) copy-start(bf16[16,2048]{1,0:T(8,128)(2,1)} %param.7) | copy-start | bytes 196612
  9.5 4.1 %copy-start.8 = (s32[16,8]{0,1:T(8,128)S(1)}, s32[16,8]{0,1:T(8,128)}, u32[]{:S(2)}) copy-start(s32[16,8]{0,1:T(8,128)} %param.9) | copy-start | bytes 1540
  9.5 23.9 %all-to-all-start.1 = ((bf16[4,1,512,384]{3,2,1,0:T(8,128)(2,1)}), bf16[4,1,512,384]{3,2,1,0:T(8,128)(2,1)S(1)}, u32[]{:S(2)}, u32[]{:S(2)}) async-start(bf16[4,1,512,384]{3,2,1,0:T(8,128)(2,1)} %stack.2), calls=%async_computation.1 | async-start | bytes 3145728 | tf_op jit(solution)/shard_map/all_to_all | solution.py:32
  19.3 36.7 %copy-start.9 = (f32[16,8]{0,1:T(8,128)S(1)}, f32[16,8]{0,1:T(8,128)}, u32[]{:S(2)}) copy-start(f32[16,8]{0,1:T(8,128)} %param.10) | copy-start | bytes 1540
  19.3 36.9 %copy-start.7 = (bf16[16,2048]{1,0:T(8,128)(2,1)S(1)}, bf16[16,2048]{1,0:T(8,128)(2,1)}, u32[]{:S(2)}) copy-start(bf16[16,2048]{1,0:T(8,128)(2,1)} %param.8) | copy-start | bytes 196612
  33.4 1.1 copy-start.3
  34.6 76.3 %all-to-all-start = ((bf16[128,2,2048]{2,1,0:T(2,128)(2,1)}), bf16[128,2,2048]{2,1,0:T(2,128)(2,1)S(1)}, u32[]{:S(2)}, u32[]{:S(2)}) async-start(bf16[128,2,2048]{2,1,0:T(2,128)(2,1)} %reshape.131), calls=%async_computation | async-start | bytes 2097152 | tf_op jit(solution)/shard_map/all_to_all | solution.py:37
  55.3 63.3 %all-gather.5.cloned.1.call-start = ((), (), s32[]{:S(2)}) async-start(), calls=%async_computation.8 | async-start | bytes 1966080 | tf_op jit(solution)/shard_map/all_gather | solution.py:30
  110.9 62.1 %all-to-all-start.3 = ((bf16[128,2,2048]{2,1,0:T(2,128)(2,1)}), bf16[128,2,2048]{2,1,0:T(2,128)(2,1)S(1)}, u32[]{:S(2)}, u32[]{:S(2)}) async-start(bf16[128,2,2048]{2,1,0:T(2,128)(2,1)} %reshape.135), calls=%async_computation.3 | async-start | bytes 2097152 | tf_op jit(solution)/shard_map/all_to_all | solution.py:50
  117.3 36.0 %all-gather.3.cloned.1.call-start = ((), (), s32[]{:S(2)}) async-start(), calls=%async_computation.7 | async-start | bytes 1966080 | tf_op jit(solution)/shard_map/all_gather | solution.py:29
  153.4 3.0 copy-start.4
  153.4 3.0 copy-start.5
  155.6 0.7 copy-start.6
  172.9 62.2 %all-to-all-start.2 = ((bf16[128,2,2048]{2,1,0:T(2,128)(2,1)}), bf16[128,2,2048]{2,1,0:T(2,128)(2,1)}, u32[]{:S(2)}, u32[]{:S(2)}) async-start(bf16[128,2,2048]{2,1,0:T(2,128)(2,1)} %reshape.133), calls=%async_computation.2 | async-start | bytes 2097152 | tf_op jit(solution)/shard_map/all_to_all | solution.py:49
  179.8 63.9 %reduce-scatter.3.cloned.1.call-start = ((), (), s32[]{:S(2)}) async-start(), calls=%async_computation.9 | async-start | bytes 1966080 | tf_op jit(solution)/shard_map/reduce_scatter | solution.py:69
  182.7 1.9 copy-start.2
  184.6 1.4 copy-start.1
  235.1 62.1 %all-to-all-start.4 = ((bf16[128,2,2048]{2,1,0:T(2,128)(2,1)}), bf16[128,2,2048]{2,1,0:T(2,128)(2,1)S(1)}, u32[]{:S(2)}, u32[]{:S(2)}) async-start(bf16[128,2,2048]{2,1,0:T(2,128)(2,1)} %reshape.137), calls=%async_computation.4 | async-start | bytes 2097152 | tf_op jit(solution)/shard_map/all_to_all | solution.py:64
  241.6 34.6 %reduce-scatter.5.cloned.1.call-start = ((), (), s32[]{:S(2)}) async-start(), calls=%async_computation.10 | async-start | bytes 1966080 | tf_op jit(solution)/shard_map/reduce_scatter | solution.py:72
Sparse Core Ops, SparseCore 0:
  58.2 33.0 all-gather.4
  120.3 33.0 all-gather.2
  184.8 31.1 reduce-scatter.2
  244.9 31.1 reduce-scatter.4
